TPU v7x, 32 devices: a whole 2x2x4 slice. The times are simulated.
32 devices in a mesh: dp: 8 (over z, y), section: 4 (over x, core).
Axes of the slice: x: 2, y: 2, z: 4, core: 2. Of those that a mesh axis runs over, the one named last changes fastest.
Arguments:
- held: bfloat16 [4, 1024, 4096], P('section', 'dp'), may hold values from -6 to 6
- norm_gain: bfloat16 [4, 1, 4096], P('section'), may hold values from 0.099609375 to 1.8984375
- w_gate: bfloat16 [4, 1, 4096, 6144], P('section', None, None, 'dp'), may hold values from -0.09375 to 0.09375
- w_up: bfloat16 [4, 1, 4096, 6144], P('section', None, None, 'dp'), may hold values from -0.09375 to 0.09375
- w_down: bfloat16 [4, 1, 6144, 4096], P('section', None, 'dp'), may hold values from -0.078125 to 0.078125
- layer_counts: int32 [4], P('section'), may hold values from 0 to 1, as said below
- query_bank: bfloat16 [128, 4096], P('dp'), may hold values from -0.099609375 to 0.099609375
- pin_bank: bfloat16 [128, 4096], P('dp'), may hold values from -0.099609375 to 0.099609375
- positive: int32 [128], P('dp'), may hold values from 0 to 127, each once
Outputs:
- section_out: bfloat16 [4, 1024, 4096], P('section', 'dp')
- grad_query: float32 [128, 4096], P('dp', 'section')
- grad_pin: float32 [128, 4096], P('dp', 'section')
Inputs may be any that keep to these rules, and one draw needn't show every extreme that they name: `layer_counts`: each section's number of applied layer slots; some section applies 1 and some section applies none. Each pin is the positive of exactly one query.
All inputs are finite; a program needn't handle non-finite values.
Results may differ from a plain program's by a relative error of at most 0.012.
Values may be sent and summed in bfloat16 or wider, within the bound.
No kernel may reach another device: no remote copies, remote signals or barrier semaphores. Data moves between devices by JAX's collectives and lax.ppermute only.
A program may use at most 128 MiB of HBM per device.

v0:
```python
import jax
import jax.numpy as jnp
from jax import lax
from jax.sharding import PartitionSpec as P

LEN = 128


INV_TEMP = 20.0
EPSILON = 1e-06


def broadcast(block, axis, source):
    block = jnp.where(lax.axis_index(axis) == source, block, jnp.zeros_like(block))
    return lax.psum(block, axis)


def rms_scaled(stream, gain_row):
    values = stream.astype(jnp.float32)
    factor = lax.rsqrt(jnp.mean(values * values, axis=-1, keepdims=True) + EPSILON)
    return (values * factor * gain_row.astype(jnp.float32)).astype(jnp.bfloat16)


def unit_rows(values):
    floats = values.astype(jnp.float32)
    length = jnp.sqrt(jnp.sum(floats * floats, axis=-1, keepdims=True) + EPSILON)
    return (floats / length, length)


def back_unit(step, unit, length):
    return (step - unit * jnp.sum(unit * step, axis=-1, keepdims=True)) / length


def make_weights(queries, targets, all_pins):
    scores = (
        lax.dot_general(
            queries, all_pins, (((1,), (1,)), ((), ())), preferred_element_type=jnp.float32
        )
        * INV_TEMP
    )
    raised = jnp.exp(scores - INV_TEMP)
    probs = raised / jnp.sum(raised, axis=1, keepdims=True)
    columns = jnp.arange(all_pins.shape[0], dtype=jnp.int32)
    onehot = (columns[None, :] == targets[:, None]).astype(jnp.float32)
    return ((probs - onehot) * INV_TEMP).astype(jnp.bfloat16)


def local(held, norm_gain, w_gate, w_up, w_down, layer_counts, query_bank, pin_bank, positive):
    rows_dev = held.shape[1]
    model_width = held.shape[2]
    seq_span = LEN // rows_dev
    layer_total = layer_counts[0]
    gains = norm_gain[0]
    gate_stack = w_gate[0]
    up_stack = w_up[0]
    down_stack = w_down[0]
    stream = held[0]
    normed = rms_scaled(stream, gains[0])
    ffn_normed = lax.all_gather(normed, "dp", axis=0, tiled=True)
    gate_out = jnp.dot(ffn_normed, gate_stack[0], preferred_element_type=jnp.float32)
    up_out = jnp.dot(ffn_normed, up_stack[0], preferred_element_type=jnp.float32)
    hidden = (jax.nn.silu(gate_out) * up_out).astype(jnp.bfloat16)
    terms = jnp.dot(hidden, down_stack[0], preferred_element_type=jnp.float32)
    update = lax.psum_scatter(
        terms.astype(jnp.bfloat16), "dp", scatter_dimension=0, tiled=True
    ).astype(jnp.float32)
    moved = (stream.astype(jnp.float32) + update).astype(jnp.bfloat16)
    stream = jnp.where(0 < layer_total, moved, stream)
    last_row = stream[rows_dev - 1 : rows_dev]
    fresh_row = broadcast(last_row, "section", lax.axis_size("section") - 1)
    holder = lax.axis_index("dp") % seq_span == seq_span - 1
    first_pin = jnp.where(holder, fresh_row, pin_bank[0:1])
    own_pins = jnp.concatenate([first_pin, pin_bank[1:]], axis=0)
    pin_unit, pin_length = unit_rows(own_pins)
    pin_send = pin_unit.astype(jnp.bfloat16)
    all_pins = lax.all_gather(pin_send, "dp", axis=0, tiled=True)
    query_unit, query_length = unit_rows(query_bank)
    query_send = query_unit.astype(jnp.bfloat16)
    weights = make_weights(query_send, positive, all_pins)
    query_step = jnp.dot(weights, all_pins, preferred_element_type=jnp.float32)
    pin_step = lax.psum_scatter(
        lax.dot_general(
            weights, query_send, (((0,), (0,)), ((), ())), preferred_element_type=jnp.float32
        ).astype(jnp.bfloat16),
        "dp",
        scatter_dimension=0,
        tiled=True,
    ).astype(jnp.float32)
    grad_query = back_unit(query_step, query_unit, query_length)
    grad_pin = back_unit(pin_step, pin_unit, pin_length)
    col_width = model_width // lax.axis_size("section")
    col_start = lax.axis_index("section") * col_width
    grad_query = lax.dynamic_slice_in_dim(grad_query, col_start, col_width, 1)
    grad_pin = lax.dynamic_slice_in_dim(grad_pin, col_start, col_width, 1)
    return (stream[None], grad_query, grad_pin)


def solution(mesh):
    return jax.shard_map(
        local,
        mesh=mesh,
        in_specs=(
            P("section", "dp", None),
            P("section", None, None),
            P("section", None, None, "dp"),
            P("section", None, None, "dp"),
            P("section", None, "dp", None),
            P("section"),
            P("dp", None),
            P("dp", None),
            P("dp"),
        ),
        out_specs=(P("section", "dp", None), P("dp", "section"), P("dp", "section")),
        check_vma=False,
    )
```

profile of v0, /device:TPU:0, one launch (start us, length us, event | category | flops | bytes accessed | tf_op | source)
XLA Modules:
  0.0 444.3 jit_solution(11333554071049897435)
XLA Ops:
  7.2 0.7 convert_element_type.69
  7.9 1.5 fusion.7
  9.5 2.5 fusion.9
  12.1 127.7 %all-gather.3.cloned.1.call-done = bf16[1024,4096]{1,0:T(8,128)(2,1)} async-done(((bf16[128,4096]{1,0:T(8,128)(2,1)}), bf16[1024,4096]{1,0:T(8,128)(2,1)}) %all-gather.3.cloned.1.call-update) | async-done | bytes 8388624 | tf_op jit(solution)/shard_map/all_gather | solution.py:59
  139.8 11.0 %fusion.1 = f32[1024,768]{1,0:T(8,128)S(1)} fusion(bf16[1024,4096]{1,0:T(8,128)(2,1)} %all-gather.3.cloned.1.call-done, bf16[1,1,4096,768]{3,2,1,0:T(8,128)(2,1)} %param.12), kind=kOutput, calls=%fused_computation.2 | convolution fusion | flops 6442450944 | bytes 17825792 | tf_op jit(solution)/shard_map/dot_general | solution.py:61
  150.9 9.9 %multiply_convert_fusion = bf16[1024,768]{1,0:T(8,128)(2,1)S(1)} fusion(f32[1024,768]{1,0:T(8,128)S(1)} %fusion.1, bf16[1024,4096]{1,0:T(8,128)(2,1)S(1)} %copy-done.6, bf16[1,1,4096,768]{3,2,1,0:T(8,128)(2,1)} %param.11), kind=kOutput, calls=%fused_computation.7 | convolution fusion | flops 6447169536 | bytes 19398656 | tf_op jit(solution)/shard_map/dot_general | solution.py:60
  160.9 8.8 %convolution_convert_fusion = bf16[1024,4096]{1,0:T(8,128)(2,1)} fusion(bf16[1024,768]{1,0:T(8,128)(2,1)S(1)} %multiply_convert_fusion, bf16[1,1,768,4096]{3,2,1,0:T(8,128)(2,1)S(1)} %bitcast.26), kind=kOutput, calls=%fused_computation | convolution fusion | flops 6446645248 | bytes 16252928 | tf_op jit(solution)/shard_map/dot_general | solution.py:63
  170.6 0.1 copy-done.4
  170.7 146.4 %reduce-scatter.3.cloned.1.call-done = bf16[128,4096]{1,0:T(8,128)(2,1)} async-done(((bf16[1024,4096]{1,0:T(8,128)(2,1)}), bf16[128,4096]{1,0:T(8,128)(2,1)}) %reduce-scatter.3.cloned.1.call-update) | async-done | bytes 1048592 | tf_op jit(solution)/shard_map/reduce_scatter | solution.py:64
  317.1 1.5 fusion.11
  318.7 11.2 %psum.7 = bf16[1,4096]{1,0:T(2,128)(2,1)S(1)} all-reduce(bf16[1,4096]{1,0:T(2,128)(2,1)S(1)} %broadcast_select_fusion), channel_id=1, replica_groups=mesh['dp'=8,'section'=4] {'section'}, use_global_device_ids=true, to_apply=%region_3.4 | all-reduce | flops 4096 | bytes 16384 | tf_op jit(solution)/shard_map/psum | solution.py:15
  329.9 0.2 fusion.15
  330.0 0.8 fusion.21
  330.8 0.0 reduce-scatter.5.cloned.1.call-start
  330.9 0.1 fusion.14
  331.0 38.3 %all-gather.5.cloned.1.call-done = bf16[128,4096]{1,0:T(8,128)(2,1)} async-done(((bf16[16,4096]{1,0:T(8,128)(2,1)}), bf16[128,4096]{1,0:T(8,128)(2,1)}) %all-gather.5.cloned.1.call-update) | async-done | bytes 1048592 | tf_op jit(solution)/shard_map/all_gather | solution.py:76
  369.3 1.9 fusion.22
  371.2 1.6 convolution_convert_fusion.1
  372.8 0.4 multiply_reduce_fusion.1
  373.2 0.7 fusion.17
  373.9 61.2 %reduce-scatter.5.cloned.1.call-done = bf16[16,4096]{1,0:T(8,128)(2,1)} async-done(((bf16[128,4096]{1,0:T(8,128)(2,1)}), bf16[16,4096]{1,0:T(8,128)(2,1)}) %reduce-scatter.5.cloned.1.call-update) | async-done | bytes 131088 | tf_op jit(solution)/shard_map/reduce_scatter | solution.py:81
  435.1 0.9 convert_element_type.68
  436.0 1.1 multiply_reduce_fusion
  437.1 0.7 fusion.16
  (30 shorter events, 0.3 us)
Async XLA Ops:
  7.2 132.7 %all-gather.3.cloned.1.call-start = ((), (), s32[]{:S(2)}) async-start(), calls=%async_computation.2 | async-start | bytes 9437184 | tf_op jit(solution)/shard_map/all_gather | solution.py:59
  12.0 305.1 %reduce-scatter.3.cloned.1.call-start = ((), (), s32[]{:S(2)}) async-start(), calls=%async_computation.3 | async-start | bytes 9437184 | tf_op jit(solution)/shard_map/reduce_scatter | solution.py:64
  139.8 11.1 %copy-start.6 = (bf16[1024,4096]{1,0:T(8,128)(2,1)S(1)}, bf16[1024,4096]{1,0:T(8,128)(2,1)}, u32[]{:S(2)}) copy-start(bf16[1024,4096]{1,0:T(8,128)(2,1)} %all-gather.3.cloned.1.call-done) | copy-start | bytes 25165828
  139.8 21.0 %slice-start = ((s8[6291456]{0:T(1024)(128)(4,1)}), s8[4194304]{0:T(1024)(128)(4,1)S(1)}, s32[]{:S(2)}) async-start(s8[6291456]{0:T(1024)(128)(4,1)} %bitcast.25), calls=%async_computation.6 | async-start | bytes 8388608
  150.9 10.0 %slice-start.1 = ((s8[6291456]{0:T(1024)(128)(4,1)}), s8[2097152]{0:T(1024)(128)(4,1)S(1)}, s32[]{:S(2)}) async-start(s8[6291456]{0:T(1024)(128)(4,1)} %bitcast.25), calls=%async_computation.7 | async-start | bytes 4194304
  169.7 0.9 copy-start.4
  169.7 147.4 %copy-start = (bf16[1,128,4096]{2,1,0:T(8,128)(2,1)S(1)}, bf16[1,128,4096]{2,1,0:T(8,128)(2,1)}, u32[]{:S(2)}) copy-start(bf16[1,128,4096]{2,1,0:T(8,128)(2,1)} %param.9) | copy-start | bytes 3145732
  169.7 161.1 %copy-start.1 = (bf16[16,4096]{1,0:T(8,128)(2,1)S(1)}, bf16[16,4096]{1,0:T(8,128)(2,1)}, u32[]{:S(2)}) copy-start(bf16[16,4096]{1,0:T(8,128)(2,1)} %param.15) | copy-start | bytes 393220
  169.8 201.4 %copy-start.5 = (s32[16]{0:T(128)S(1)}, s32[16]{0:T(128)}, u32[]{:S(2)}) copy-start(s32[16]{0:T(128)} %param.17) | copy-start | bytes 196
  169.8 199.5 %all-gather.5.cloned.1.call-start = ((), (), s32[]{:S(2)}) async-start(), calls=%async_computation.4 | async-start | bytes 1179648 | tf_op jit(solution)/shard_map/all_gather | solution.py:76
  318.6 54.6 %copy-start.2 = (bf16[128,4096]{1,0:T(8,128)(2,1)}, bf16[128,4096]{1,0:T(8,128)(2,1)S(1)}, u32[]{:S(2)}) copy-start(bf16[128,4096]{1,0:T(8,128)(2,1)S(1)} %fusion.11) | copy-start | bytes 3145732
  330.8 104.3 %reduce-scatter.5.cloned.1.call-start = ((), (), s32[]{:S(2)}) async-start(), calls=%async_computation.5 | async-start | bytes 1179648 | tf_op jit(solution)/shard_map/reduce_scatter | solution.py:81
  369.3 3.5 copy-start.3
Sparse Core Ops, SparseCore 0:
  12.2 127.6 all-gather.2
  169.9 147.1 reduce-scatter.2
  330.9 38.3 all-gather.4
  373.0 62.1 reduce-scatter.4
where the time goes:
time: 445 us; the launch traced here: 444 us
  waiting for transfers between devices  374 us (84%)
  matrix products  33.7 us (8%)
  between operations  14.7 us (3%)
  blocking collectives  11.2 us (3%)
  other arithmetic  10.9 us (2%)
    reduce_scatter x1, waiting for transfers between devices, local(): lax.psum_scatter(terms.astype(jnp.bfloat16), 'dp', scatter_dimension=0, t...  146 us
    all_gather x1, waiting for transfers between devices, local(): ffn_normed = lax.all_gather(normed, 'dp', axis=0, tiled=True)  128 us
    reduce_scatter x1, waiting for transfers between devices, local(): lax.psum_scatter(lax.dot_general(weights, query_send, (((0,), (0,)), ((),...  61.2 us
    all_gather x1, waiting for transfers between devices, local(): all_pins = lax.all_gather(pin_send, 'dp', axis=0, tiled=True)  38.3 us
    psum x1, blocking collectives, broadcast(): return lax.psum(block, axis)  11.2 us
    dot_general x1, matrix products, local(): jnp.dot(ffn_normed, up_stack[0], preferred_element_type=jnp.float32)  11 us
    dot_general x1, matrix products, local(): jnp.dot(ffn_normed, gate_stack[0], preferred_element_type=jnp.float32)  9.94 us
  transfers between devices with their start and end apart: 4, of which 4 were waited for; matrix products, arithmetic and copies ran while one was open for 0% of the time, Pallas kernels for 0%

commit v1 on v0

v1 whole, which is shorter than its diff:
```python
import functools

import jax
import jax.numpy as jnp
from jax import lax
from jax.experimental import pallas as pl
from jax.experimental.pallas import tpu as pltpu
from jax.sharding import PartitionSpec as P

INV_TEMP = 20.0
EPSILON = 1e-06
BOTH = ("dp", "section")
ANYWHERE = pl.BlockSpec(memory_space=pl.ANY)
IN_VMEM = pl.BlockSpec(memory_space=pltpu.VMEM)


def ring_order(size):
    return list(range(0, size, 2)) + list(range(size - 1, 0, -2))


def rms_scaled(stream, gain_row):
    values = stream.astype(jnp.float32)
    factor = lax.rsqrt(jnp.mean(values * values, axis=-1, keepdims=True) + EPSILON)
    return (values * factor * gain_row.astype(jnp.float32)).astype(jnp.bfloat16)


def unit_rows(values):
    floats = values.astype(jnp.float32)
    length = jnp.sqrt(jnp.sum(floats * floats, axis=-1, keepdims=True) + EPSILON)
    return (floats / length, length)


def add(*values):
    return sum(v.astype(jnp.float32) for v in values).astype(jnp.bfloat16)


def copies_in(pieces, tokens, sems):
    rows = pieces[0].shape[0]
    copies = [
        pltpu.make_async_copy(piece, tokens.at[pl.ds(i * rows, rows)], sems.at[i])
        for i, piece in enumerate(pieces)
    ]
    for copy in copies:
        copy.start()
    return copies


def copies_out(result, outs, sems):
    rows = outs[0].shape[0]
    copies = [
        pltpu.make_async_copy(result.at[pl.ds(i * rows, rows)], out, sems.at[i])
        for i, out in enumerate(outs)
    ]
    for copy in copies:
        copy.start()
    for copy in copies:
        copy.wait()


def gated(tokens, gate, up, hidden):
    gate_out = jnp.dot(tokens[...], gate[...], preferred_element_type=jnp.float32)
    up_out = jnp.dot(tokens[...], up[...], preferred_element_type=jnp.float32)
    hidden[...] = (gate_out / (1 + jnp.exp(-gate_out)) * up_out).astype(jnp.bfloat16)


def lowered(hidden, down, result):
    result[...] = jnp.dot(hidden[...], down[...], preferred_element_type=jnp.float32).astype(
        jnp.bfloat16
    )


def first_kernel(count, *refs):
    pieces, weights, refs = refs[:count], refs[count : count + 3], refs[count + 3 :]
    outs, kept, refs = refs[:count], refs[count : count + 3], refs[count + 3 :]
    tokens, hidden, result, in_sems, out_sems, weight_sems = refs
    loads = copies_in(pieces, tokens, in_sems)
    fetches = [
        pltpu.make_async_copy(weight, keep, weight_sems.at[i])
        for i, (weight, keep) in enumerate(zip(weights, kept))
    ]
    for copy in fetches:
        copy.start()
    for copy in loads + fetches[:2]:
        copy.wait()
    gated(tokens, kept[0], kept[1], hidden)
    fetches[2].wait()
    lowered(hidden, kept[2], result)
    copies_out(result, outs, out_sems)


def next_kernel(count, *refs):
    pieces, weights, refs = refs[:count], refs[count : count + 3], refs[count + 3 :]
    outs, refs = refs[:count], refs[count:]
    tokens, hidden, result, in_sems, out_sems = refs
    for copy in copies_in(pieces, tokens, in_sems):
        copy.wait()
    gated(tokens, weights[0], weights[1], hidden)
    lowered(hidden, weights[2], result)
    copies_out(result, outs, out_sems)


def multiply(pieces, weights, keep):
    count = len(pieces)
    rows, width = pieces[0].shape
    units = weights[0].shape[1]
    scratch = [
        pltpu.VMEM((count * rows, width), jnp.bfloat16),
        pltpu.VMEM((count * rows, units), jnp.bfloat16),
        pltpu.VMEM((count * rows, width), jnp.bfloat16),
        pltpu.SemaphoreType.DMA((count,)),
        pltpu.SemaphoreType.DMA((count,)),
    ]
    out_shape = [jax.ShapeDtypeStruct(p.shape, jnp.bfloat16) for p in pieces]
    params = pltpu.CompilerParams(vmem_limit_bytes=20 << 20)
    cost = pl.CostEstimate(flops=1 << 20, bytes_accessed=1 << 20, transcendentals=0)
    if keep:
        outs = pl.pallas_call(
            functools.partial(first_kernel, count),
            out_shape=out_shape + [pltpu.VMEM(w.shape, w.dtype) for w in weights],
            in_specs=[ANYWHERE] * (count + 3),
            out_specs=[ANYWHERE] * count + [IN_VMEM] * 3,
            scratch_shapes=scratch + [pltpu.SemaphoreType.DMA((3,))],
            compiler_params=params,
            cost_estimate=cost,
        )(*pieces, *weights)
        return tuple(outs[:count]), outs[count:]
    weights = [pltpu.with_memory_space_constraint(w, pltpu.VMEM) for w in weights]
    return pl.pallas_call(
        functools.partial(next_kernel, count),
        out_shape=out_shape,
        in_specs=[ANYWHERE] * count + [IN_VMEM] * 3,
        out_specs=[ANYWHERE] * count,
        scratch_shapes=scratch,
        compiler_params=params,
        cost_estimate=cost,
    )(*pieces, *weights)


def local(held, norm_gain, w_gate, w_up, w_down, layer_counts, query_bank, pin_bank, positive):
    replicas = lax.axis_size("dp")
    sections = lax.axis_size("section")
    rows_dev, model_width = held.shape[1:]
    pair_dev = query_bank.shape[0]
    half = replicas // 2
    cut = rows_dev // 2
    order = ring_order(replicas)
    place = [order.index(replica) for replica in range(replicas)]
    ring = [(order[i], order[(i + 1) % replicas]) for i in range(replicas)]
    ring_back = [(b, a) for a, b in ring]
    me = lax.axis_index("dp")
    section = lax.axis_index("section")
    position = jnp.array(place, jnp.int32)[me]
    last = sections - 1
    active = layer_counts[0] > 0
    stream = held[0]
    col_width = model_width // sections
    col_start = section * col_width

    def forward(values):
        return lax.ppermute(values, "dp", ring)

    def backward(values):
        return lax.ppermute(values, "dp", ring_back)

    def own_columns(values):
        return lax.dynamic_slice_in_dim(values, col_start, col_width, 1)

    def gathered(values):
        reach = 1
        while reach < replicas:
            other = lax.ppermute(values, "dp", [(i, i ^ reach) for i in range(replicas)])
            lower = (me & reach) == 0
            values = jnp.concatenate(
                [jnp.where(lower, values, other), jnp.where(lower, other, values)], axis=1
            )
            reach *= 2
        return values

    def added_up(values):
        reach = 1
        while reach < replicas:
            pairs = [(i * sections + last, (i ^ reach) * sections + last) for i in range(replicas)]
            values = values + lax.ppermute(values, BOTH, pairs)
            reach *= 2
        return values

    def with_held(rows):
        rows = jnp.concatenate([rows, rows]).astype(jnp.float32)
        rows = lax.dynamic_slice_in_dim(rows, replicas - position, replicas, 0)
        mine = jnp.arange(replicas)[:, None] == position
        return rows + jnp.where(mine, stream[rows_dev - 1 :].astype(jnp.float32), 0.0)

    query_unit, query_length = unit_rows(query_bank)
    query_send = query_unit.astype(jnp.bfloat16)
    pin_unit, pin_length = unit_rows(pin_bank)
    pin_send = pin_unit.astype(jnp.bfloat16)
    own_targets = jnp.zeros((pair_dev, col_width), jnp.bfloat16)
    own_targets = own_targets.at[:, 0].set(positive.astype(jnp.bfloat16))
    own_sends = jnp.stack([own_columns(query_send), own_columns(pin_send), own_targets])

    def gather_and_multiply(own_sends):
        normed = rms_scaled(stream, norm_gain[0])
        f_top, f_low = normed[:cut], normed[cut:]
        b_top, b_low = f_top, f_low
        f_top, b_low = forward(f_top), backward(b_low)
        f_low, b_top = forward(f_low), backward(b_top)
        own, weights = multiply(
            [normed[:cut], normed[cut:]], [w_gate[0, 0], w_up[0, 0], w_down[0, 0]], True
        )
        terms_f, terms_b = [], []
        for step in range(1, half):
            arrived = [f_top, f_low, b_top, b_low]
            f_top, b_low = forward(f_top), backward(b_low)
            if step < half - 1:
                f_low, b_top = forward(f_low), backward(b_top)
            terms = multiply(arrived, weights, False)
            terms_f.append(terms[:2])
            terms_b.append(terms[2:])
        f_low, b_top = forward(terms_b[-1][1]), backward(terms_f[-1][0])
        far = multiply([f_top, b_low], weights, False)
        f_top, b_low = forward(far[0]), backward(far[1])
        in_order = [own] + terms_b + [far] + terms_f[::-1]
        rows = jnp.concatenate([t[1][cut - 1 :] for t in in_order])
        fresh = added_up(with_held(rows)).astype(jnp.bfloat16)
        sends = gathered(own_sends)
        return own, tuple(terms_f), tuple(terms_b), (f_top, f_low, b_top, b_low), fresh, sends

    def gather_only(own_sends):
        fresh = added_up(with_held(jnp.zeros((replicas, model_width), jnp.float32)))
        empty = jnp.zeros((cut, model_width), jnp.bfloat16)
        some = tuple((empty, empty) for _ in range(1, half))
        return (
            (empty, empty),
            some,
            some,
            (empty,) * 4,
            fresh.astype(jnp.bfloat16),
            gathered(own_sends),
        )

    own, terms_f, terms_b, moving, fresh, sends = lax.cond(
        active, gather_and_multiply, gather_only, own_sends
    )

    targets = sends[2, :, 0].astype(jnp.int32)
    pairs = sends.shape[1]
    message = jnp.concatenate(
        [sends[0], sends[1], fresh.reshape(replicas * sections, col_width)]
    )
    messages = [message] + [
        lax.ppermute(message, "section", [(s, (s - step) % sections) for s in range(sections)])
        for step in range(1, sections)
    ]

    def reduce_middle(moving):
        f_top, f_low, b_top, b_low = moving
        for distance in range(half - 1, 1, -1):
            to_f, to_b = terms_b[distance - 1], terms_f[distance - 1]
            if distance < half - 1:
                f_low, b_top = forward(add(to_f[1], f_low)), backward(add(to_b[0], b_top))
            f_top, b_low = forward(add(to_f[0], f_top)), backward(add(to_b[1], b_low))
        return f_top, f_low, b_top, b_low

    moving = lax.cond(active, reduce_middle, lambda moving: moving, moving)

    def loss(messages):
        fresh_rows = sum(
            jnp.where(section == (last - step) % sections, message[2 * pairs :], 0)
            for step, message in enumerate(messages)
        ).reshape(replicas, model_width)
        fresh_rows = jnp.stack([fresh_rows[place[replica]] for replica in range(replicas)])
        fresh_unit, fresh_length = unit_rows(fresh_rows)
        fresh_send = fresh_unit.astype(jnp.bfloat16)
        turned = lax.dynamic_slice_in_dim(
            jnp.concatenate([fresh_send, fresh_send], axis=1), col_start, model_width, 1
        )
        queries = jnp.concatenate([m[:pairs] for m in messages], axis=1)
        pins = jnp.concatenate([m[pairs : 2 * pairs] for m in messages], axis=1)
        pins = pins.reshape(replicas, pair_dev, model_width)
        pins = jnp.concatenate([turned[:, None], pins[:, 1:]], axis=1).reshape(-1, model_width)
        cosines = lax.dot_general(
            queries, pins, (((1,), (1,)), ((), ())), preferred_element_type=jnp.float32
        )
        raised = jnp.exp(INV_TEMP * cosines - INV_TEMP)
        probs = raised / jnp.sum(raised, axis=1, keepdims=True)
        columns = jnp.arange(pairs, dtype=jnp.int32)
        onehot = (columns[None, :] == targets[:, None]).astype(jnp.float32)
        weights = ((probs - onehot) * INV_TEMP).astype(jnp.bfloat16)
        row_start = me * pair_dev
        dots = weights.astype(jnp.float32) * cosines
        query_weights = lax.dynamic_slice_in_dim(weights, row_start, pair_dev, 0)
        pin_weights = lax.dynamic_slice_in_dim(weights, row_start, pair_dev, 1)
        query_dot = lax.dynamic_slice_in_dim(jnp.sum(dots, axis=1), row_start, pair_dev, 0)
        pin_dot = lax.dynamic_slice_in_dim(jnp.sum(dots, axis=0), row_start, pair_dev, 0)
        query_step = jnp.dot(
            query_weights, pins[:, :col_width], preferred_element_type=jnp.float32
        )
        pin_step = lax.dot_general(
            pin_weights,
            queries[:, :col_width],
            (((0,), (0,)), ((), ())),
            preferred_element_type=jnp.float32,
        )
        own_unit = lax.dynamic_slice_in_dim(fresh_unit, me, 1, 0)
        own_length = lax.dynamic_slice_in_dim(fresh_length, me, 1, 0)
        own_unit = jnp.concatenate([own_columns(own_unit), own_columns(pin_unit)[1:]])
        own_length = jnp.concatenate([own_length, pin_length[1:]])
        grad_query = (query_step - own_columns(query_unit) * query_dot[:, None]) / query_length
        grad_pin = (pin_step - own_unit * pin_dot[:, None]) / own_length
        return grad_query, grad_pin

    def reduce_last(moving, messages):
        f_top, f_low, b_top, b_low = moving
        to_f, to_b = terms_b[0], terms_f[0]
        f_low, b_top = forward(add(to_f[1], f_low)), backward(add(to_b[0], b_top))
        f_top, b_low = forward(add(to_f[0], f_top)), backward(add(to_b[1], b_low))
        grads = loss(messages)
        top = add(stream[:cut], own[0], f_top, b_top)
        low = add(stream[cut:], own[1], f_low, b_low)
        return jnp.concatenate([top, low]), *grads

    def keep_stream(moving, messages):
        return stream, *loss(messages)

    stream, grad_query, grad_pin = lax.cond(active, reduce_last, keep_stream, moving, messages)
    return (stream[None], grad_query, grad_pin)


def solution(mesh):
    return jax.shard_map(
        local,
        mesh=mesh,
        in_specs=(
            P("section", "dp", None),
            P("section", None, None),
            P("section", None, None, "dp"),
            P("section", None, None, "dp"),
            P("section", None, "dp", None),
            P("section"),
            P("dp", None),
            P("dp", None),
            P("dp"),
        ),
        out_specs=(P("section", "dp", None), P("dp", "section"), P("dp", "section")),
        check_vma=False,
    )
```

time: 445 us -> 229 us (0.51)
  waiting for transfers between devices: 374 us -> 67.6 us
  starting transfers between devices: 0.16 us -> 48.6 us
  Pallas kernels: 0 us -> 35.8 us
  local copies, waits for them, and re-layouts: 0.14 us -> 32.6 us
  matrix products: 33.7 us -> 2.86 us
  other arithmetic: 10.9 us -> 37 us
  between operations: 14.7 us -> 1.45 us
  blocking collectives: 11.2 us -> 0 us
    reduce_scatter x2 -> x0, waiting for transfers between devices: 208 us -> none  [the longest x1 146 us: local(): lax.psum_scatter(terms.astype(jnp.bfloat16), 'dp', scatter_dimension=0, t...]
    all_gather x2 -> x0, waiting for transfers between devices: 166 us -> none  [the longest x1 128 us: local(): ffn_normed = lax.all_gather(normed, 'dp', axis=0, tiled=True)]
    ppermute x0 -> x37, waiting for transfers between devices: none -> 67.6 us  [the longest x14 29 us: forward(): return lax.ppermute(values, 'dp', ring)]
    ppermute x0 -> x37, starting transfers between devices: none -> 48.6 us  [the longest x14 22.9 us: forward(): return lax.ppermute(values, 'dp', ring)]
    pallas_call x0 -> x5, Pallas kernels: none -> 35.8 us  [the longest x4 27.2 us: multiply(): pl.pallas_call(functools.partial(next_kernel, count), out_shape=out_shape...]
    dot_general x6 -> x3, matrix products: 33.7 us -> 2.86 us  [the longest x1 1.57 us: loss(): lax.dot_general(queries, pins, (((1,), (1,)), ((), ())), preferred_elemen...]
    another operation x0 -> x17, local copies, waits for them, and re-layouts: none -> 19 us
    convert_element_type x2 -> x13, other arithmetic: 1.68 us -> 20.2 us  [the longest x11 19 us: add(): return sum((v.astype(jnp.float32) for v in values)).astype(jnp.bfloat16)]
  transfers between devices with their start and end apart: 4 -> 37, of which waited for: 4 -> 13; matrix products, arithmetic and copies ran while one was open for 0% -> 16% of each run, Pallas kernels for 0% -> 16%
where the time goes in v1:
time: 229 us; the launch traced here: 227 us
  waiting for transfers between devices  67.6 us (30%)
  starting transfers between devices  48.6 us (21%)
  other arithmetic  37 us (16%)
  Pallas kernels  35.8 us (16%)
  local copies, waits for them, and re-layouts  32.6 us (14%)
  matrix products  2.86 us (1%)
    ppermute x14, waiting for transfers between devices, forward(): return lax.ppermute(values, 'dp', ring)  29 us
    pallas_call x4, Pallas kernels, multiply(): pl.pallas_call(functools.partial(next_kernel, count), out_shape=out_shape...  27.2 us
    ppermute x14, starting transfers between devices, forward(): return lax.ppermute(values, 'dp', ring)  22.9 us
    convert_element_type x11, other arithmetic, add(): return sum((v.astype(jnp.float32) for v in values)).astype(jnp.bfloat16)  19 us
    another operation x15, local copies, waits for them, and re-layouts  18.8 us
    ppermute x3, waiting for transfers between devices, local(): lax.ppermute(message, 'section', [(s, (s - step) % sections) for s in ran...  17.4 us
    ppermute x14, waiting for transfers between devices, backward(): return lax.ppermute(values, 'dp', ring_back)  15.7 us
    ppermute x14, starting transfers between devices, backward(): return lax.ppermute(values, 'dp', ring_back)  9.98 us
  transfers between devices with their start and end apart: 37, of which 13 were waited for; matrix products, arithmetic and copies ran while one was open for 16% of the time, Pallas kernels for 16%

profile of v1, /device:TPU:0, one launch (start us, length us, event | category | flops | bytes accessed | tf_op | source)
XLA Modules:
  0.0 227.5 jit_solution(16846146013879153167)
XLA Ops:
  7.5 136.5 %conditional.5 = (bf16[64,4096]{1,0:T(8,128)(2,1)}, bf16[64,4096]{1,0:T(8,128)(2,1)}, bf16[64,4096]{1,0:T(8,128)(2,1)}, bf16[64,4096]{1,0:T(8,128)(2,1)}, bf16[6...) conditional(s32[]{:T(128)} %bitcast.22, (s32[]{:T(128)}, ...), branch_computations={%region_3.4_spmd, %region_4.6_spmd} | conditional | flops 14918418 | bytes 214077568
  10.7 3.1 %collective-permute-start.6 = (bf16[64,4096]{1,0:T(8,128)(2,1)S(1)}, bf16[64,4096]{1,0:T(8,128)(2,1)S(1)}, u32[]{:S(2)}, u32[]{:S(2)}) collective-permute-start(bf16[64,4096]{1,0:T(8,128)(2,1)S(1)} %get-tuple-element.490.refs_0_), channel_id=1, source_target_pairs={{0,8},{8,16},{16,24},{24,28},{28,20},{20,12},{12,4},{4,0},{1,9},{9... | collective-permute-start | bytes 1572872 | tf_op jit(solution)/shard_map/cond/branch_1_fun/ppermute | solution.py:160
  15.8 6.7 %collective-permute-done.6.refs_0_ = bf16[64,4096]{1,0:T(8,128)(2,1)S(1)} collective-permute-done((bf16[64,4096]{1,0:T(8,128)(2,1)S(1)}, bf16[64,4096]{1,0:T(8,128)(2,1)S(1)}, u32[]{:S(2)}, u32[]{:S(2)}) %collective-permute-start.6) | collective-permute-done | bytes 524320 | tf_op jit(solution)/shard_map/cond/branch_1_fun/ppermute | solution.py:160
  25.0 7.0 %collective-permute-done.7.refs_1_ = bf16[64,4096]{1,0:T(8,128)(2,1)S(1)} collective-permute-done((bf16[64,4096]{1,0:T(8,128)(2,1)S(1)}, bf16[64,4096]{1,0:T(8,128)(2,1)S(1)}, u32[]{:S(2)}, u32[]{:S(2)}) %collective-permute-start.7) | collective-permute-done | bytes 524320 | tf_op jit(solution)/shard_map/cond/branch_1_fun/ppermute | solution.py:160
  34.5 3.5 %collective-permute-done.10.refs_0_ = bf16[64,4096]{1,0:T(8,128)(2,1)S(1)} collective-permute-done((bf16[64,4096]{1,0:T(8,128)(2,1)S(1)}, bf16[64,4096]{1,0:T(8,128)(2,1)S(1)}, u32[]{:S(2)}, u32[]{:S(2)}) %collective-permute-start.10) | collective-permute-done | bytes 524320 | tf_op jit(solution)/shard_map/cond/branch_1_fun/ppermute | solution.py:160
  38.0 3.7 %collective-permute-start.14 = (bf16[64,4096]{1,0:T(8,128)(2,1)S(1)}, bf16[64,4096]{1,0:T(8,128)(2,1)}, u32[]{:S(2)}, u32[]{:S(2)}) collective-permute-start(bf16[64,4096]{1,0:T(8,128)(2,1)S(1)} %collective-permute-done.10.refs_0_), channel_id=1, source_target_pairs={{0,8},{8,16},{16,24},{24,28},{28,20},{20,12},{12,4},{4,0},{1,9},{9... | collective-permute-start | bytes 1572872 | tf_op jit(solution)/shard_map/cond/branch_1_fun/ppermute | solution.py:160
  44.1 5.5 %collective-permute-done.24 = bf16[3,16,1024]{2,1,0:T(8,128)(2,1)S(1)} collective-permute-done((bf16[3,16,1024]{2,1,0:T(8,128)(2,1)S(1)}, bf16[3,16,1024]{2,1,0:T(8,128)(2,1)S(1)}, u32[]{:S(2)}, u32[]{:S(2)}) %collective-permute-start.24) | collective-permute-done | bytes 98336 | tf_op jit(solution)/shard_map/cond/branch_1_fun/ppermute | solution.py:171
  55.8 8.6 %branch_1_fun.5 = (bf16[64,4096]{1,0:T(8,128)(2,1)}, bf16[64,4096]{1,0:T(8,128)(2,1)}, bf16[4096,768]{1,0:T(8,128)(2,1)S(1)}, bf16[4096,768]{1,0:T(8,128)(2,1)S(1)}, bf16[768,4096]{1,0:T(8,128)(2,1)S(1)}) custom-call(bf16[64,4096]{1,0:T(8,128)(2,1)S(1)} %get-tuple-element.490.refs_0_, bf16[64,4096]{1,0:T(8,128)(2,1)S(1)} %get-tuple-element.489.refs_1_, ...), custom_call_target="tpu_custom_call" | custom-call | flops 1048576 | bytes 1048576 | tf_op jit(solution)/shard_map/cond/branch_1_fun/pallas_call | solution.py:117
  76.5 3.4 %collective-permute-start.26 = (bf16[3,64,1024]{2,1,0:T(8,128)(2,1)S(1)}, bf16[3,64,1024]{2,1,0:T(8,128)(2,1)S(1)}, u32[]{:S(2)}, u32[]{:S(2)}) collective-permute-start(bf16[3,64,1024]{2,1,0:T(8,128)(2,1)S(1)} %pad_maximum_fusion.9), channel_id=1, source_target_pairs={{0,16},{4,20},{8,24},{12,28},{16,0},{20,4},{24,8},{28,12},{1,17},{... | collective-permute-start | bytes 1179656 | tf_op jit(solution)/shard_map/cond/branch_1_fun/ppermute | solution.py:171
  79.9 2.8 %copy-done.1 = bf16[4096,768]{1,0:T(8,128)(2,1)S(1)} copy-done((bf16[4096,768]{1,0:T(8,128)(2,1)S(1)}, bf16[4096,768]{1,0:T(8,128)(2,1)}, u32[]{:S(2)}) %copy-start.1) | copy-done | bytes 6291480 | tf_op jit(solution)/shard_map/conditional.1
  82.7 2.8 %copy-done.3 = bf16[4096,768]{1,0:T(8,128)(2,1)S(1)} copy-done((bf16[4096,768]{1,0:T(8,128)(2,1)S(1)}, bf16[4096,768]{1,0:T(8,128)(2,1)}, u32[]{:S(2)}) %copy-start.3) | copy-done | bytes 6291480 | tf_op jit(solution)/shard_map/conditional.1
  88.3 7.5 %branch_1_fun.6 = (bf16[64,4096]{1,0:T(8,128)(2,1)}, bf16[64,4096]{1,0:T(8,128)(2,1)}, bf16[64,4096]{1,0:T(8,128)(2,1)}, bf16[64,4096]{1,0:T(8,128)(2,1)}) custom-call(bf16[64,4096]{1,0:T(8,128)(2,1)S(1)} %collective-permute-done.6.refs_0_, bf16[64,4096]{1,0:T(8,128)(2,1)S(1)} %collective-permute-done.7.refs_1_, ...), custom_call_target="tpu_custom_call" | custom-call | flops 1048576 | bytes 1048576 | tf_op jit(solution)/shard_map/cond/branch_1_fun/pallas_call | solution.py:128
  97.5 8.0 %branch_1_fun.7 = (bf16[64,4096]{1,0:T(8,128)(2,1)}, bf16[64,4096]{1,0:T(8,128)(2,1)}, bf16[64,4096]{1,0:T(8,128)(2,1)}, bf16[64,4096]{1,0:T(8,128)(2,1)}) custom-call(bf16[64,4096]{1,0:T(8,128)(2,1)S(1)} %collective-permute-done.10.refs_0_, bf16[64,4096]{1,0:T(8,128)(2,1)} %collective-permute-done.11.refs_1_, ...), custom_call_target="tpu_custom_call" | custom-call | flops 1048576 | bytes 1048576 | tf_op jit(solution)/shard_map/cond/branch_1_fun/pallas_call | solution.py:128
  107.3 7.6 %branch_1_fun.8 = (bf16[64,4096]{1,0:T(8,128)(2,1)S(1)}, bf16[64,4096]{1,0:T(8,128)(2,1)}, bf16[64,4096]{1,0:T(8,128)(2,1)}, bf16[64,4096]{1,0:T(8,128)(2,1)S(1)}) custom-call(bf16[64,4096]{1,0:T(8,128)(2,1)} %collective-permute-done.14.refs_0_, bf16[64,4096]{1,0:T(8,128)(2,1)} %collective-permute-done.15.refs_1_, ...), custom_call_target="tpu_custom_call" | custom-call | flops 1048576 | bytes 1048576 | tf_op jit(solution)/shard_map/cond/branch_1_fun/pallas_call | solution.py:128
  115.9 4.0 %branch_1_fun.9 = (bf16[64,4096]{1,0:T(8,128)(2,1)S(1)}, bf16[64,4096]{1,0:T(8,128)(2,1)S(1)}) custom-call(bf16[64,4096]{1,0:T(8,128)(2,1)} %collective-permute-done.18.refs_0_, bf16[64,4096]{1,0:T(8,128)(2,1)} %collective-permute-done.19.refs_1_, bf16[4096,768]{1,0:T(8,128)(2,1)S(1)} %copy-done.1, bf16[4096,768]{1,0:T(8,128)(2,1)S(1)} %copy-done.3, ...), custom_call_target="tpu_custom_call" | custom-call | flops 1048576 | bytes 1048576 | tf_op jit(solution)/shard_map/cond/branch_1_fun/pallas_call | solution.py:128
  131.2 5.2 %collective-permute-done.21 = bf16[64,4096]{1,0:T(8,128)(2,1)} collective-permute-done((bf16[64,4096]{1,0:T(8,128)(2,1)S(1)}, bf16[64,4096]{1,0:T(8,128)(2,1)}, u32[]{:S(2)}, u32[]{:S(2)}) %collective-permute-start.21) | collective-permute-done | bytes 524320 | tf_op jit(solution)/shard_map/cond/branch_1_fun/ppermute | solution.py:160
  136.4 5.6 %collective-permute-done.20 = bf16[64,4096]{1,0:T(8,128)(2,1)} collective-permute-done((bf16[64,4096]{1,0:T(8,128)(2,1)S(1)}, bf16[64,4096]{1,0:T(8,128)(2,1)}, u32[]{:S(2)}, u32[]{:S(2)}) %collective-permute-start.20) | collective-permute-done | bytes 524320 | tf_op jit(solution)/shard_map/cond/branch_1_fun/ppermute | solution.py:160
  144.7 7.9 %collective-permute-start.40 = (bf16[288,1024]{1,0:T(8,128)(2,1)S(1)}, bf16[288,1024]{1,0:T(8,128)(2,1)S(1)}, u32[]{:S(2)}, u32[]{:S(2)}) collective-permute-start(bf16[288,1024]{1,0:T(8,128)(2,1)S(1)} %constant_dynamic-update-slice_fusion), channel_id=1, source_target_pairs={{0,3},{1,0},{2,1},{3,2},{4,7},{5,4},{6,5},{7,6},{8,11},{9,8},{10,9... | collective-permute-start | bytes 1769480 | tf_op jit(solution)/shard_map/ppermute | solution.py:251
  152.5 30.6 %conditional.6 = ((bf16[64,4096]{1,0:T(8,128)(2,1)}, bf16[64,4096]{1,0:T(8,128)(2,1)}, bf16[64,4096]{1,0:T(8,128)(2,1)}, bf16[64,4096]{1,0:T(8,128)(2,1)})) conditional(s32[]{:T(128)} %bitcast.22, (bf16[64,4096]{1,0:T(8,128)(2,1)}, bf16[64,4096]{1,0:T(8,128)(2,1)}, bf16[64,4096]{1,0:T(8,128)(2,1)}, bf16[64,4096]{1,0:T(8,128)(2,1)}) %tuple.50, ...), branch_computations={%region_6.7_spmd, %region_7.8_spmd} | conditional | flops 6291456 | bytes 22020376 | solution.py:264
  164.9 7.8 %collective-permute-done.4 = bf16[64,4096]{1,0:T(8,128)(2,1)S(1)} collective-permute-done((bf16[64,4096]{1,0:T(8,128)(2,1)S(1)}, bf16[64,4096]{1,0:T(8,128)(2,1)S(1)}, u32[]{:S(2)}, u32[]{:S(2)}) %collective-permute-start.4) | collective-permute-done | bytes 524320 | tf_op jit(solution)/shard_map/cond/branch_1_fun/ppermute | solution.py:163
  175.3 7.9 %collective-permute-done.5 = bf16[64,4096]{1,0:T(8,128)(2,1)} collective-permute-done((bf16[64,4096]{1,0:T(8,128)(2,1)S(1)}, bf16[64,4096]{1,0:T(8,128)(2,1)}, u32[]{:S(2)}, u32[]{:S(2)}) %collective-permute-start.5) | collective-permute-done | bytes 524320 | tf_op jit(solution)/shard_map/cond/branch_1_fun/ppermute | solution.py:163
  183.2 16.3 %collective-permute-done.41 = bf16[288,1024]{1,0:T(8,128)(2,1)S(1)} collective-permute-done((bf16[288,1024]{1,0:T(8,128)(2,1)S(1)}, bf16[288,1024]{1,0:T(8,128)(2,1)S(1)}, u32[]{:S(2)}, u32[]{:S(2)}) %collective-permute-start.41) | collective-permute-done | bytes 589856 | tf_op jit(solution)/shard_map/ppermute | solution.py:251
  200.6 26.2 %conditional.7 = (bf16[128,4096]{1,0:T(8,128)(2,1)}, f32[16,1024]{1,0:T(8,128)S(1)}, f32[16,1024]{1,0:T(8,128)S(1)}) conditional(s32[]{:T(128)} %bitcast.22, (bf16[288,1024]{1,0:T(8,128)(2,1)S(1)}, bf16[288,1024]{1,0:T(8,128)(2,1)S(1)}, bf16[288,1024]{1,0:T(8,128)(2,1)S(1)}, bf16[128,1024]{1,0:T(8,128)(2,1)S(1)}, s32[]{:T(128)}, ...), branch_computations={%region_8.13_spmd, %region_13.18_spmd} | conditional | flops 164494992 | bytes 35862064 | solution.py:325
  223.0 2.8 %add_convert_fusion.9 = (bf16[64,4096]{1,0:T(8,128)(2,1)S(1)}, bf16[64,4096]{1,0:T(8,128)(2,1)S(1)}) fusion(bf16[64,4096]{1,0:T(8,128)(2,1)} %collective-permute-done.31, bf16[64,4096]{1,0:T(8,128)(2,1)} %collective-permute-done.30, bf16[64,4096]{1,0:T(8,128)(2,1)} %get-tuple-element.259, bf16[128,4096]{1,0:T(8,128)(2,1)} %get-tuple-element.258, ...), kind=kLoop, calls=%fused_computation.71 | loop fusion | flops 4194304 | bytes 5242880 | tf_op jit(solution)/shard_map/cond/branch_1_fun/convert_element_type | solution.py:34
  (187 shorter events, 96.9 us)
Async XLA Ops:
  13.7 18.3 %collective-permute-start.7 = (bf16[64,4096]{1,0:T(8,128)(2,1)S(1)}, bf16[64,4096]{1,0:T(8,128)(2,1)S(1)}, u32[]{:S(2)}, u32[]{:S(2)}) collective-permute-start(bf16[64,4096]{1,0:T(8,128)(2,1)S(1)} %get-tuple-element.489.refs_1_), channel_id=1, source_target_pairs={{0,8},{8,16},{16,24},{24,28},{28,20},{20,12},{12,4},{4,0},{1,9},{9... | collective-permute-start | bytes 1572872 | tf_op jit(solution)/shard_map/cond/branch_1_fun/ppermute | solution.py:160
  15.8 18.7 %collective-permute-start.8 = (bf16[64,4096]{1,0:T(8,128)(2,1)S(1)}, bf16[64,4096]{1,0:T(8,128)(2,1)}, u32[]{:S(2)}, u32[]{:S(2)}) collective-permute-start(bf16[64,4096]{1,0:T(8,128)(2,1)S(1)} %get-tuple-element.490.refs_0_), channel_id=1, source_target_pairs={{8,0},{16,8},{24,16},{28,24},{20,28},{12,20},{4,12},{0,4},{9,1},{1... | collective-permute-start | bytes 1572872 | tf_op jit(solution)/shard_map/cond/branch_1_fun/ppermute | solution.py:163
  22.5 15.4 %collective-permute-start.10 = (bf16[64,4096]{1,0:T(8,128)(2,1)S(1)}, bf16[64,4096]{1,0:T(8,128)(2,1)S(1)}, u32[]{:S(2)}, u32[]{:S(2)}) collective-permute-start(bf16[64,4096]{1,0:T(8,128)(2,1)S(1)} %collective-permute-done.6.refs_0_), channel_id=1, source_target_pairs={{0,8},{8,16},{16,24},{24,28},{28,20},{20,12},{12,4},{4,0},{1,9},{9... | collective-permute-start | bytes 1572872 | tf_op jit(solution)/shard_map/cond/branch_1_fun/ppermute | solution.py:160
  25.0 16.7 %collective-permute-start.13 = (bf16[64,4096]{1,0:T(8,128)(2,1)S(1)}, bf16[64,4096]{1,0:T(8,128)(2,1)}, u32[]{:S(2)}, u32[]{:S(2)}) collective-permute-start(bf16[64,4096]{1,0:T(8,128)(2,1)S(1)} %collective-permute-done.9.refs_3_), channel_id=1, source_target_pairs={{8,0},{16,8},{24,16},{28,24},{20,28},{12,20},{4,12},{0,4},{9,1},{1... | collective-permute-start | bytes 1572872 | tf_op jit(solution)/shard_map/cond/branch_1_fun/ppermute | solution.py:163
  32.0 18.4 %collective-permute-start.11 = (bf16[64,4096]{1,0:T(8,128)(2,1)S(1)}, bf16[64,4096]{1,0:T(8,128)(2,1)}, u32[]{:S(2)}, u32[]{:S(2)}) collective-permute-start(bf16[64,4096]{1,0:T(8,128)(2,1)S(1)} %collective-permute-done.7.refs_1_), channel_id=1, source_target_pairs={{0,8},{8,16},{16,24},{24,28},{28,20},{20,12},{12,4},{4,0},{1,9},{9... | collective-permute-start | bytes 1572872 | tf_op jit(solution)/shard_map/cond/branch_1_fun/ppermute | solution.py:160
  34.5 17.9 %collective-permute-start.12 = (bf16[64,4096]{1,0:T(8,128)(2,1)}, bf16[64,4096]{1,0:T(8,128)(2,1)}, u32[]{:S(2)}, u32[]{:S(2)}) collective-permute-start(bf16[64,4096]{1,0:T(8,128)(2,1)} %collective-permute-done.8.refs_2_), channel_id=1, source_target_pairs={{8,0},{16,8},{24,16},{28,24},{20,28},{12,20},{4,12},{0,4},{9,1},{1... | collective-permute-start | bytes 1572872 | tf_op jit(solution)/shard_map/cond/branch_1_fun/ppermute | solution.py:163
  38.0 14.9 %collective-permute-start.14 = (bf16[64,4096]{1,0:T(8,128)(2,1)S(1)}, bf16[64,4096]{1,0:T(8,128)(2,1)}, u32[]{:S(2)}, u32[]{:S(2)}) collective-permute-start(bf16[64,4096]{1,0:T(8,128)(2,1)S(1)} %collective-permute-done.10.refs_0_), channel_id=1, source_target_pairs={{0,8},{8,16},{16,24},{24,28},{28,20},{20,12},{12,4},{4,0},{1,9},{9... | collective-permute-start | bytes 1572872 | tf_op jit(solution)/shard_map/cond/branch_1_fun/ppermute | solution.py:160
  41.7 13.2 %collective-permute-start.17 = (bf16[64,4096]{1,0:T(8,128)(2,1)}, bf16[64,4096]{1,0:T(8,128)(2,1)}, u32[]{:S(2)}, u32[]{:S(2)}) collective-permute-start(bf16[64,4096]{1,0:T(8,128)(2,1)} %collective-permute-done.13.refs_3_), channel_id=1, source_target_pairs={{8,0},{16,8},{24,16},{28,24},{20,28},{12,20},{4,12},{0,4},{9,1},{1... | collective-permute-start | bytes 1572872 | tf_op jit(solution)/shard_map/cond/branch_1_fun/ppermute | solution.py:163
  50.3 25.1 %collective-permute-start.25 = (bf16[3,32,1024]{2,1,0:T(8,128)(2,1)}, bf16[3,32,1024]{2,1,0:T(8,128)(2,1)}, u32[]{:S(2)}, u32[]{:S(2)}) collective-permute-start(bf16[3,32,1024]{2,1,0:T(8,128)(2,1)} %pad_maximum_fusion.10), channel_id=1, source_target_pairs={{0,8},{4,12},{8,0},{12,4},{16,24},{20,28},{24,16},{28,20},{1,9},{5... | collective-permute-start | bytes 589832 | tf_op jit(solution)/shard_map/cond/branch_1_fun/ppermute | solution.py:171
  50.3 56.9 %collective-permute-start.15 = (bf16[64,4096]{1,0:T(8,128)(2,1)}, bf16[64,4096]{1,0:T(8,128)(2,1)}, u32[]{:S(2)}, u32[]{:S(2)}) collective-permute-start(bf16[64,4096]{1,0:T(8,128)(2,1)} %collective-permute-done.11.refs_1_), channel_id=1, source_target_pairs={{0,8},{8,16},{16,24},{24,28},{28,20},{20,12},{12,4},{4,0},{1,9},{9... | collective-permute-start | bytes 1572872 | tf_op jit(solution)/shard_map/cond/branch_1_fun/ppermute | solution.py:160
  52.4 54.9 %collective-permute-start.16 = (bf16[64,4096]{1,0:T(8,128)(2,1)}, bf16[64,4096]{1,0:T(8,128)(2,1)}, u32[]{:S(2)}, u32[]{:S(2)}) collective-permute-start(bf16[64,4096]{1,0:T(8,128)(2,1)} %collective-permute-done.12.refs_2_), channel_id=1, source_target_pairs={{8,0},{16,8},{24,16},{28,24},{20,28},{12,20},{4,12},{0,4},{9,1},{1... | collective-permute-start | bytes 1572872 | tf_op jit(solution)/shard_map/cond/branch_1_fun/ppermute | solution.py:163
  52.9 62.9 %collective-permute-start.18 = (bf16[64,4096]{1,0:T(8,128)(2,1)}, bf16[64,4096]{1,0:T(8,128)(2,1)}, u32[]{:S(2)}, u32[]{:S(2)}) collective-permute-start(bf16[64,4096]{1,0:T(8,128)(2,1)} %collective-permute-done.14.refs_0_), channel_id=1, source_target_pairs={{0,8},{8,16},{16,24},{24,28},{28,20},{20,12},{12,4},{4,0},{1,9},{9... | collective-permute-start | bytes 1572872 | tf_op jit(solution)/shard_map/cond/branch_1_fun/ppermute | solution.py:160
  54.9 61.0 %collective-permute-start.19 = (bf16[64,4096]{1,0:T(8,128)(2,1)}, bf16[64,4096]{1,0:T(8,128)(2,1)}, u32[]{:S(2)}, u32[]{:S(2)}) collective-permute-start(bf16[64,4096]{1,0:T(8,128)(2,1)} %collective-permute-done.17.refs_3_), channel_id=1, source_target_pairs={{8,0},{16,8},{24,16},{28,24},{20,28},{12,20},{4,12},{0,4},{9,1},{1... | collective-permute-start | bytes 1572872 | tf_op jit(solution)/shard_map/cond/branch_1_fun/ppermute | solution.py:163
  76.5 45.2 %collective-permute-start.26 = (bf16[3,64,1024]{2,1,0:T(8,128)(2,1)S(1)}, bf16[3,64,1024]{2,1,0:T(8,128)(2,1)S(1)}, u32[]{:S(2)}, u32[]{:S(2)}) collective-permute-start(bf16[3,64,1024]{2,1,0:T(8,128)(2,1)S(1)} %pad_maximum_fusion.9), channel_id=1, source_target_pairs={{0,16},{4,20},{8,24},{12,28},{16,0},{20,4},{24,8},{28,12},{1,17},{... | collective-permute-start | bytes 1179656 | tf_op jit(solution)/shard_map/cond/branch_1_fun/ppermute | solution.py:171
  129.1 12.9 %collective-permute-start.23 = (bf16[64,4096]{1,0:T(8,128)(2,1)S(1)}, bf16[64,4096]{1,0:T(8,128)(2,1)}, u32[]{:S(2)}, u32[]{:S(2)}) collective-permute-start(bf16[64,4096]{1,0:T(8,128)(2,1)S(1)} %get-tuple-element.229), channel_id=1, source_target_pairs={{8,0},{16,8},{24,16},{28,24},{20,28},{12,20},{4,12},{0,4},{9,1},{1... | collective-permute-start | bytes 1572872 | tf_op jit(solution)/shard_map/cond/branch_1_fun/ppermute | solution.py:163
  129.2 12.8 %collective-permute-start.20 = (bf16[64,4096]{1,0:T(8,128)(2,1)S(1)}, bf16[64,4096]{1,0:T(8,128)(2,1)}, u32[]{:S(2)}, u32[]{:S(2)}) collective-permute-start(bf16[64,4096]{1,0:T(8,128)(2,1)S(1)} %get-tuple-element.226), channel_id=1, source_target_pairs={{0,8},{8,16},{16,24},{24,28},{28,20},{20,12},{12,4},{4,0},{1,9},{9... | collective-permute-start | bytes 1572872 | tf_op jit(solution)/shard_map/cond/branch_1_fun/ppermute | solution.py:160
  144.7 38.5 %collective-permute-start.40 = (bf16[288,1024]{1,0:T(8,128)(2,1)S(1)}, bf16[288,1024]{1,0:T(8,128)(2,1)S(1)}, u32[]{:S(2)}, u32[]{:S(2)}) collective-permute-start(bf16[288,1024]{1,0:T(8,128)(2,1)S(1)} %constant_dynamic-update-slice_fusion), channel_id=1, source_target_pairs={{0,3},{1,0},{2,1},{3,2},{4,7},{5,4},{6,5},{7,6},{8,11},{9,8},{10,9... | collective-permute-start | bytes 1769480 | tf_op jit(solution)/shard_map/ppermute | solution.py:251
  155.8 19.5 %collective-permute-start.2 = (bf16[64,4096]{1,0:T(8,128)(2,1)S(1)}, bf16[64,4096]{1,0:T(8,128)(2,1)}, u32[]{:S(2)}, u32[]{:S(2)}) collective-permute-start(bf16[64,4096]{1,0:T(8,128)(2,1)S(1)} %add_convert_fusion.3), channel_id=1, source_target_pairs={{0,8},{8,16},{16,24},{24,28},{28,20},{20,12},{12,4},{4,0},{1,9},{9... | collective-permute-start | bytes 1572872 | tf_op jit(solution)/shard_map/cond/branch_1_fun/ppermute | solution.py:160
  157.8 17.5 %collective-permute-start.3 = (bf16[64,4096]{1,0:T(8,128)(2,1)S(1)}, bf16[64,4096]{1,0:T(8,128)(2,1)}, u32[]{:S(2)}, u32[]{:S(2)}) collective-permute-start(bf16[64,4096]{1,0:T(8,128)(2,1)S(1)} %add_convert_fusion.2), channel_id=1, source_target_pairs={{8,0},{16,8},{24,16},{28,24},{20,28},{12,20},{4,12},{0,4},{9,1},{1... | collective-permute-start | bytes 1572872 | tf_op jit(solution)/shard_map/cond/branch_1_fun/ppermute | solution.py:163
  183.2 16.3 %collective-permute-start.41 = (bf16[288,1024]{1,0:T(8,128)(2,1)S(1)}, bf16[288,1024]{1,0:T(8,128)(2,1)S(1)}, u32[]{:S(2)}, u32[]{:S(2)}) collective-permute-start(bf16[288,1024]{1,0:T(8,128)(2,1)S(1)} %constant_dynamic-update-slice_fusion), channel_id=1, source_target_pairs={{0,2},{1,3},{2,0},{3,1},{4,6},{5,7},{6,4},{7,5},{8,10},{9,11},{10,... | collective-permute-start | bytes 1769480 | tf_op jit(solution)/shard_map/ppermute | solution.py:251
  183.2 17.4 %collective-permute-start.42 = (bf16[288,1024]{1,0:T(8,128)(2,1)S(1)}, bf16[288,1024]{1,0:T(8,128)(2,1)S(1)}, u32[]{:S(2)}, u32[]{:S(2)}) collective-permute-start(bf16[288,1024]{1,0:T(8,128)(2,1)S(1)} %constant_dynamic-update-slice_fusion), channel_id=1, source_target_pairs={{0,1},{1,2},{2,3},{3,0},{4,5},{5,6},{6,7},{7,4},{8,9},{9,10},{10,1... | collective-permute-start | bytes 1769480 | tf_op jit(solution)/shard_map/ppermute | solution.py:251
  202.7 20.2 %collective-permute-start.31 = (bf16[64,4096]{1,0:T(8,128)(2,1)}, bf16[64,4096]{1,0:T(8,128)(2,1)}, u32[]{:S(2)}, u32[]{:S(2)}) collective-permute-start(bf16[64,4096]{1,0:T(8,128)(2,1)} %add_convert_fusion.10), channel_id=1, source_target_pairs={{8,0},{16,8},{24,16},{28,24},{20,28},{12,20},{4,12},{0,4},{9,1},{1... | collective-permute-start | bytes 1572872 | tf_op jit(solution)/shard_map/cond/branch_1_fun/ppermute | solution.py:163
  206.2 16.7 %collective-permute-start.30 = (bf16[64,4096]{1,0:T(8,128)(2,1)}, bf16[64,4096]{1,0:T(8,128)(2,1)}, u32[]{:S(2)}, u32[]{:S(2)}) collective-permute-start(bf16[64,4096]{1,0:T(8,128)(2,1)} %add_convert_fusion.11), channel_id=1, source_target_pairs={{0,8},{8,16},{16,24},{24,28},{28,20},{20,12},{12,4},{4,0},{1,9},{9... | collective-permute-start | bytes 1572872 | tf_op jit(solution)/shard_map/cond/branch_1_fun/ppermute | solution.py:160
  209.0 13.9 %collective-permute-start.33 = (bf16[64,4096]{1,0:T(8,128)(2,1)}, bf16[64,4096]{1,0:T(8,128)(2,1)}, u32[]{:S(2)}, u32[]{:S(2)}) collective-permute-start(bf16[64,4096]{1,0:T(8,128)(2,1)} %add_convert_fusion.7), channel_id=1, source_target_pairs={{8,0},{16,8},{24,16},{28,24},{20,28},{12,20},{4,12},{0,4},{9,1},{1... | collective-permute-start | bytes 1572872 | tf_op jit(solution)/shard_map/cond/branch_1_fun/ppermute | solution.py:163
  (32 other events, 301.9 us)
